TPU v7x, 32 devices: a whole 2x2x4 slice. The times are simulated.
32 devices in a mesh: blk: 8 (over z, y), uly: 4 (over x, core).
Axes of the slice: x: 2, y: 2, z: 4, core: 2. Of those that a mesh axis runs over, the one named last changes fastest.
Arguments:
- queries: bfloat16 [1536, 2560], P(('blk', 'uly')), may hold values from -30 to 30
- keys: bfloat16 [1536, 2560], P(('blk', 'uly')), may hold values from -4 to 4
- values: bfloat16 [1536, 2560], P(('blk', 'uly')), may hold values from -6 to 6
Outputs:
- attended: bfloat16 [1536, 2560], P(('blk', 'uly'))
All inputs are finite; a program needn't handle non-finite values.
Results may differ from a plain program's by a relative error of at most 0.0049.
Values may be sent and summed in bfloat16 or wider, within the bound.
A program may use at most 192 MiB of HBM per device.

v0:
```python
import jax
import jax.numpy as jnp
from jax import lax
from jax.sharding import PartitionSpec as P

HEAD_DIM = 128


def fold_step(carry, heads_q, piece):
    running_max, running_total, running_sum = carry
    key_rows, value_rows = piece
    count = key_rows.shape[0]
    nheads = heads_q.shape[1]
    key_heads = key_rows.reshape(count, nheads, HEAD_DIM)
    value_heads = value_rows.reshape(count, nheads, HEAD_DIM)
    scores = jnp.einsum(
        "qhd,khd->qhk", heads_q, key_heads, preferred_element_type=jnp.float32
    ) * HEAD_DIM ** (-0.5)
    new_max = jnp.maximum(running_max, jnp.max(scores, axis=2))
    probs = jnp.exp(scores - new_max[:, :, None])
    new_total = jnp.sum(probs, axis=2)
    weights = probs.astype(jnp.bfloat16)
    added = jnp.einsum("qhk,khd->qhd", weights, value_heads, preferred_element_type=jnp.float32)
    return (new_max, new_total, added)


def start_carry(rows, nheads):
    return (
        jnp.full((rows, nheads), -1e30, jnp.float32),
        jnp.zeros((rows, nheads), jnp.float32),
        jnp.zeros((rows, nheads, HEAD_DIM), jnp.float32),
    )


def per_device(queries, keys, values):
    local_q, local_k, local_v = (
        lax.all_to_all(queries, "uly", split_axis=1, concat_axis=0, tiled=True),
        lax.all_to_all(keys, "uly", split_axis=1, concat_axis=0, tiled=True),
        lax.all_to_all(values, "uly", split_axis=1, concat_axis=0, tiled=True),
    )
    rows = local_q.shape[0]
    nheads = local_q.shape[1] // HEAD_DIM
    heads_q = local_q.reshape(rows, nheads, HEAD_DIM)
    final_max, final_total, final_sum = fold_step(
        start_carry(rows, nheads),
        heads_q,
        (
            lax.all_gather(local_k, "blk", axis=0, tiled=True),
            lax.all_gather(local_v, "blk", axis=0, tiled=True),
        ),
    )
    result = (
        (final_sum / final_total[:, :, None]).reshape(rows, nheads * HEAD_DIM).astype(jnp.bfloat16)
    )
    return lax.all_to_all(result, "uly", split_axis=0, concat_axis=1, tiled=True)


def solution(mesh):
    return jax.shard_map(
        per_device,
        mesh=mesh,
        in_specs=(P(("blk", "uly"), None), P(("blk", "uly"), None), P(("blk", "uly"), None)),
        out_specs=P(("blk", "uly"), None),
        check_vma=False,
    )
```

profile of v0, /device:TPU:0, one launch (start us, length us, event | category | flops | bytes accessed | tf_op | source)
XLA Modules:
  0.0 137.7 jit_solution(10980874076199178882)
XLA Ops:
  6.5 0.0 all-gather.3.cloned.1.call-start
  6.5 1.0 copy.45
  7.5 10.0 %all_to_all.70 = bf16[48,4,640]{2,0,1:T(8,128)(2,1)} all-to-all(bf16[48,4,640]{2,0,1:T(8,128)(2,1)S(1)} %bitcast.54), channel_id=1, replica_groups=mesh['blk'=8,'uly'=4] {'uly'}, dimensions={1} | all-to-all | bytes 491520 | tf_op jit(solution)/shard_map/all_to_all | solution.py:38
  17.5 0.0 all-gather.3.cloned.1.call-update
  17.5 0.0 all-gather.5.cloned.1.call-start
  17.6 1.0 copy.44
  18.5 8.9 %all_to_all.71 = bf16[48,4,640]{2,0,1:T(8,128)(2,1)} all-to-all(bf16[48,4,640]{2,0,1:T(8,128)(2,1)S(1)} %bitcast.55), channel_id=1, replica_groups=mesh['blk'=8,'uly'=4] {'uly'}, dimensions={1} | all-to-all | bytes 491520 | tf_op jit(solution)/shard_map/all_to_all | solution.py:39
  27.5 0.0 all-gather.5.cloned.1.call-update
  27.5 1.0 copy.46
  28.5 8.2 %all_to_all.72 = bf16[48,4,640]{2,0,1:T(8,128)(2,1)S(1)} all-to-all(bf16[48,4,640]{2,0,1:T(8,128)(2,1)S(1)} %bitcast.56), channel_id=1, replica_groups=mesh['blk'=8,'uly'=4] {'uly'}, dimensions={1} | all-to-all | bytes 491520 | tf_op jit(solution)/shard_map/all_to_all | solution.py:37
  36.7 0.3 reshape.30
  37.0 28.9 %all-gather.3.cloned.1.call-done = bf16[1536,640]{1,0:T(8,128)(2,1)} async-done(((bf16[192,640]{1,0:T(8,128)(2,1)}), bf16[1536,640]{1,0:T(8,128)(2,1)}) %all-gather.3.cloned.1.call-update) | async-done | bytes 1966096 | tf_op jit(solution)/shard_map/all_gather | solution.py:48
  65.9 2.7 %copy.22 = bf16[1536,640]{0,1:T(8,128)(2,1)S(1)} copy(bf16[1536,640]{1,0:T(8,128)(2,1)} %all-gather.3.cloned.1.call-done) | data formatting | bytes 3932160 | tf_op jit(solution)/shard_map/all_gather | solution.py:48
  68.6 1.0 bitcast_reduce_fusion
  69.6 0.0 copy-start
  69.6 2.5 %copy-done = f32[5,1536,192]{1,2,0:T(8,128)} copy-done((f32[5,1536,192]{1,2,0:T(8,128)}, f32[5,1536,192]{1,2,0:T(8,128)S(1)}, u32[]{:S(2)}) %copy-start) | copy-done | bytes 5898264
  72.1 1.1 fusion.1
  73.3 41.5 %all-gather.5.cloned.1.call-done = bf16[1536,640]{1,0:T(8,128)(2,1)} async-done(((bf16[192,640]{1,0:T(8,128)(2,1)}), bf16[1536,640]{1,0:T(8,128)(2,1)}) %all-gather.5.cloned.1.call-update) | async-done | bytes 1966096 | tf_op jit(solution)/shard_map/all_gather | solution.py:49
  114.7 2.7 %copy.27 = bf16[1536,640]{0,1:T(8,128)(2,1)S(1)} copy(bf16[1536,640]{1,0:T(8,128)(2,1)} %all-gather.5.cloned.1.call-done) | data formatting | bytes 3932160 | tf_op jit(solution)/shard_map/all_gather | solution.py:49
  117.4 3.8 %fusion.13 = bf16[192,5,128]{2,0,1:T(8,128)(2,1)S(1)} fusion(bf16[1536,5,128]{0,2,1:T(8,128)(2,1)S(1)} %bitcast.49, f32[5,1536,192]{1,2,0:T(8,128)} %copy-done, f32[192,5]{0,1:T(8,128)S(1)} %broadcast_maximum_fusion, f32[192,5]{0,1:T(8,128)S(1)} %fusion.1), kind=kOutput, calls=%fused_computation.10 | convolution fusion | flops 382156800 | bytes 8117760 | tf_op jit(solution)/shard_map/qhk,khd->qhd/dot_general | solution.py:23
  121.2 0.2 copy.29
  121.4 0.3 convert_element_type.12
  121.7 8.4 %all_to_all.73 = bf16[4,48,640]{2,1,0:T(8,128)(2,1)S(1)} all-to-all(bf16[4,48,640]{2,1,0:T(8,128)(2,1)S(1)} %convert_element_type.12), channel_id=1, replica_groups=mesh['blk'=8,'uly'=4] {'uly'}, dimensions={0} | all-to-all | bytes 491520 | tf_op jit(solution)/shard_map/all_to_all | solution.py:55
  130.1 0.7 copy.36
  (1 shorter events, 0.0 us)
Async XLA Ops:
  6.5 59.4 %all-gather.3.cloned.1.call-start = ((), (), s32[]{:S(2)}) async-start(), calls=%async_computation.4 | async-start | bytes 2211840 | tf_op jit(solution)/shard_map/all_gather | solution.py:48
  17.5 97.2 %all-gather.5.cloned.1.call-start = ((), (), s32[]{:S(2)}) async-start(), calls=%async_computation.5 | async-start | bytes 2211840 | tf_op jit(solution)/shard_map/all_gather | solution.py:49
  69.6 2.5 %copy-start = (f32[5,1536,192]{1,2,0:T(8,128)}, f32[5,1536,192]{1,2,0:T(8,128)S(1)}, u32[]{:S(2)}) copy-start(f32[5,1536,192]{1,2,0:T(8,128)S(1)} %get-tuple-element.6) | copy-start | bytes 17694724
Sparse Core Ops, SparseCore 0:
  17.6 48.2 all-gather.2
  68.1 46.5 all-gather.4
where the time goes:
time: 138 us
  waiting for transfers between devices  70.4 us (51%)
  blocking collectives  35.6 us (26%)
  between operations  13.5 us (10%)
  local copies, waits for them, and re-layouts  12.3 us (9%)
  matrix products  4.81 us (3%)
    all_gather x1, waiting for transfers between devices, per_device(): lax.all_gather(local_v, 'blk', axis=0, tiled=True)  41.5 us
    all_gather x1, waiting for transfers between devices, per_device(): lax.all_gather(local_k, 'blk', axis=0, tiled=True)  28.9 us
    all_to_all x1, blocking collectives, per_device(): lax.all_to_all(keys, 'uly', split_axis=1, concat_axis=0, tiled=True)  9.98 us
    all_to_all x1, blocking collectives, per_device(): lax.all_to_all(values, 'uly', split_axis=1, concat_axis=0, tiled=True)  8.93 us
    all_to_all x1, blocking collectives, per_device(): lax.all_to_all(result, 'uly', split_axis=0, concat_axis=1, tiled=True)  8.4 us
    all_to_all x1, blocking collectives, per_device(): lax.all_to_all(queries, 'uly', split_axis=1, concat_axis=0, tiled=True)  8.24 us
    dot_general x1, matrix products, fold_step(): jnp.einsum('qhk,khd->qhd', weights, value_heads, preferred_element_type=j...  3.8 us
  transfers between devices with their start and end apart: 2, of which 2 were waited for; matrix products, arithmetic and copies ran while one was open for 5% of the time, Pallas kernels for 0%

commit v1 on v0

v1 whole, which is shorter than its diff:
```python
import functools

import jax
import jax.numpy as jnp
from jax import lax
from jax.experimental import pallas as pl
from jax.experimental.pallas import tpu as pltpu
from jax.sharding import PartitionSpec as P

HEAD_DIM = 128
GROUPS = 4
MESH = pl.DeviceIdType.MESH
LOG2E = 1.4426950408889634


def attend_kernel(q_in, k_in, v_in, out, q_buf, kv, acc, tot, top, o_buf, z_send, q_recv, z_recv,
                  x_send, x_recv, y_send, y_recv, s_send, s_recv, d_send, dk_recv, dv_recv,
                  own_sem, o_send, o_recv):
    rows, features = q_in.shape
    cols = features // GROUPS
    heads = cols // HEAD_DIM
    b, u = lax.axis_index("blk"), lax.axis_index("uly")
    z, y = b // 2, b % 2
    x, c = u // 2, u % 2

    def plane(j):
        return lax.rem(z + j + GROUPS, GROUPS)

    def column(index):
        return pl.ds(pl.multiple_of(index * cols, HEAD_DIM), cols)

    x_peer = (b, 2 * (1 - x) + c)
    y_peer = (2 * z + 1 - y, u)
    sibling = (b, 2 * x + 1 - c)

    def z_peer(j):
        return (2 * plane(j) + y, u)

    barrier = pltpu.get_barrier_semaphore()
    peers = [z_peer(1), z_peer(2), z_peer(3), x_peer, y_peer, sibling]
    for peer in peers:
        pl.semaphore_signal(barrier, inc=1, device_id=peer, device_id_type=MESH)
    pl.semaphore_wait(barrier, len(peers))

    sends = []

    def send(src, dst, send_sem, recv_sem, peer):
        copy = pltpu.make_async_remote_copy(
            src_ref=src, dst_ref=dst, send_sem=send_sem, recv_sem=recv_sem,
            device_id=peer, device_id_type=MESH)
        copy.start()
        sends.append(copy)

    def landed(ref, sem):
        pltpu.make_async_copy(ref, ref, sem).wait()

    def slot(s):
        return pl.ds(s * rows, rows)

    for j in range(1, GROUPS):
        to = column(plane(j))
        send(q_in.at[:, to], q_buf.at[slot(j)], z_send.at[3 * j], q_recv.at[j], z_peer(j))
        send(k_in.at[:, to], kv.at[j, 0, slot(0)], z_send.at[3 * j + 1], z_recv.at[j], z_peer(j))
        send(v_in.at[:, to], kv.at[j, 1, slot(0)], z_send.at[3 * j + 2], z_recv.at[j], z_peer(j))
    mine = column(z)
    own = [
        pltpu.make_async_copy(q_in.at[:, mine], q_buf.at[slot(0)], own_sem.at[0]),
        pltpu.make_async_copy(k_in.at[:, mine], kv.at[0, 0, slot(0)], own_sem.at[1]),
        pltpu.make_async_copy(v_in.at[:, mine], kv.at[0, 1, slot(0)], own_sem.at[2]),
    ]
    for copy in own:
        copy.start()

    def stage1(j):
        if j == 0:
            for copy in own:
                copy.wait()
        else:
            landed(kv.at[j, :, slot(0)], z_recv.at[j])
        block = kv.at[j, :, slot(0)]
        send(block, kv.at[j, :, slot(1)], x_send.at[j], x_recv.at[j], x_peer)
        send(block, kv.at[j, :, slot(2)], y_send.at[j], y_recv.at[j], y_peer)
        send(block, kv.at[j, :, slot(4)], s_send.at[4 * j], s_recv.at[j], sibling)

    def stage2(j):
        landed(kv.at[j, :, slot(1)], x_recv.at[j])
        send(kv.at[j, 0, slot(1)], kv.at[j, 0, slot(3)], d_send.at[2 * j], dk_recv.at[j], y_peer)
        send(kv.at[j, :, slot(1)], kv.at[j, :, slot(5)], s_send.at[4 * j + 1], s_recv.at[j], sibling)
        landed(kv.at[j, :, slot(2)], y_recv.at[j])
        send(kv.at[j, 1, slot(2)], kv.at[j, 1, slot(3)], d_send.at[2 * j + 1], dv_recv.at[j], x_peer)
        send(kv.at[j, :, slot(2)], kv.at[j, :, slot(6)], s_send.at[4 * j + 2], s_recv.at[j], sibling)

    def stage3(j):
        landed(kv.at[j, 0, slot(3)], dk_recv.at[j])
        landed(kv.at[j, 1, slot(3)], dv_recv.at[j])
        send(kv.at[j, :, slot(3)], kv.at[j, :, slot(7)], s_send.at[4 * j + 3], s_recv.at[j], sibling)

    def fold(j):
        if j == 0:
            for i in range(1, GROUPS):
                landed(q_buf.at[slot(i)], q_recv.at[i])
        landed(kv.at[j, :, pl.ds(4 * rows, 4 * rows)], s_recv.at[j])
        for h in range(heads):
            lanes = slice(h * HEAD_DIM, (h + 1) * HEAD_DIM)
            scores = lax.dot_general(
                q_buf[:, lanes], kv[j, 0, :, lanes], (((1,), (1,)), ((), ())),
                preferred_element_type=jnp.float32) * (LOG2E * HEAD_DIM ** -0.5)
            peak = jnp.max(scores, axis=1, keepdims=True)
            if j > 0:
                before = top[:, h:h + 1]
                peak = jnp.maximum(before, peak)
                shrink = jnp.exp2(before - peak)
            probs = jnp.exp2(scores - peak)
            part = jnp.sum(probs, axis=1, keepdims=True)
            added = jnp.dot(probs.astype(jnp.bfloat16), kv[j, 1, :, lanes],
                            preferred_element_type=jnp.float32)
            if j > 0:
                part = part + shrink * tot[:, h:h + 1]
                added = added + shrink * acc[:, lanes]
            if j < GROUPS - 1:
                top[:, h:h + 1] = peak
                tot[:, h:h + 1] = part
                acc[:, lanes] = added
            else:
                o_buf[:, lanes] = (added / part).astype(jnp.bfloat16)

    stage1(0)
    stage2(0)
    stage1(1)
    stage3(0)
    stage2(1)
    fold(0)
    stage1(2)
    stage3(1)
    stage2(2)
    fold(1)
    stage1(3)
    stage3(2)
    stage2(3)
    fold(2)
    stage3(3)
    fold(3)

    for j in range(1, GROUPS):
        send(o_buf.at[slot(j)], out.at[:, mine], o_send.at[j], o_recv.at[j], z_peer(-j))
    keep = pltpu.make_async_copy(o_buf.at[slot(0)], out.at[:, mine], own_sem.at[0])
    keep.start()
    keep.wait()
    for j in range(1, GROUPS):
        landed(out.at[:, column(plane(j))], o_recv.at[j])
    for copy in sends:
        copy.wait_send()


def attend(queries, keys, values):
    rows, features = queries.shape
    cols = features // GROUPS
    heads = cols // HEAD_DIM
    queries_here = GROUPS * rows
    dma = pltpu.SemaphoreType.DMA
    flops = 4 * queries_here * cols * 32 * rows
    return pl.pallas_call(
        attend_kernel,
        out_shape=jax.ShapeDtypeStruct((rows, features), jnp.bfloat16),
        in_specs=[pl.BlockSpec(memory_space=pl.ANY)] * 3,
        out_specs=pl.BlockSpec(memory_space=pl.ANY),
        scratch_shapes=[
            pltpu.VMEM((queries_here, cols), jnp.bfloat16),
            pltpu.VMEM((GROUPS, 2, 8 * rows, cols), jnp.bfloat16),
            pltpu.VMEM((queries_here, cols), jnp.float32),
            pltpu.VMEM((queries_here, HEAD_DIM), jnp.float32),
            pltpu.VMEM((queries_here, HEAD_DIM), jnp.float32),
            pltpu.VMEM((queries_here, cols), jnp.bfloat16),
            dma((12,)), dma((4,)), dma((4,)),
            dma((4,)), dma((4,)), dma((4,)), dma((4,)),
            dma((16,)), dma((4,)), dma((8,)), dma((4,)), dma((4,)),
            dma((3,)), dma((4,)), dma((4,)),
        ],
        compiler_params=pltpu.CompilerParams(
            collective_id=0, has_side_effects=True, vmem_limit_bytes=40 * 2**20),
        cost_estimate=pl.CostEstimate(flops=flops, bytes_accessed=8 * rows * features, transcendentals=0),
    )(queries, keys, values)


def attend_any(queries, keys, values):
    def to_heads(array):
        return lax.all_to_all(array, "uly", split_axis=1, concat_axis=0, tiled=True)

    heads_q, heads_k, heads_v = to_heads(queries), to_heads(keys), to_heads(values)
    all_k = lax.all_gather(heads_k, "blk", axis=0, tiled=True)
    all_v = lax.all_gather(heads_v, "blk", axis=0, tiled=True)

    def split(array):
        return array.reshape(array.shape[0], -1, HEAD_DIM)

    scores = jnp.einsum("qhd,khd->qhk", split(heads_q), split(all_k),
                        preferred_element_type=jnp.float32) * HEAD_DIM ** (-0.5)
    probs = jnp.exp(scores - jnp.max(scores, axis=2, keepdims=True))
    total = jnp.sum(probs, axis=2)
    summed = jnp.einsum("qhk,khd->qhd", probs.astype(jnp.bfloat16), split(all_v),
                        preferred_element_type=jnp.float32)
    result = (summed / total[:, :, None]).reshape(heads_q.shape).astype(jnp.bfloat16)
    return lax.all_to_all(result, "uly", split_axis=0, concat_axis=1, tiled=True)


def solution(mesh):
    spec = P(("blk", "uly"), None)
    small = mesh.shape["blk"] == 2 * GROUPS and mesh.shape["uly"] == 4
    return jax.shard_map(
        attend if small else attend_any,
        mesh=mesh,
        in_specs=(spec, spec, spec),
        out_specs=spec,
        check_vma=False,
    )
```

time: 138 us -> 53.3 us (0.39)
  waiting for transfers between devices: 70.4 us -> 0 us
  Pallas kernels: 0 us -> 49.5 us
  blocking collectives: 35.6 us -> 0 us
  between operations: 13.5 us -> 0.01 us
  local copies, waits for them, and re-layouts: 12.3 us -> 3.53 us
  matrix products: 4.81 us -> 0 us
    all_gather x2 -> x0, waiting for transfers between devices: 70.4 us -> none  [the longest x1 41.5 us: per_device(): lax.all_gather(local_v, 'blk', axis=0, tiled=True)]
    pallas_call x0 -> x1, Pallas kernels: none -> 49.5 us  [attend(): pl.pallas_call(attend_kernel, out_shape=jax.ShapeDtypeStruct((rows, featu...]
    all_to_all x4 -> x0, blocking collectives: 35.6 us -> none  [the longest x1 9.98 us: per_device(): lax.all_to_all(keys, 'uly', split_axis=1, concat_axis=0, tiled=True)]
    all_gather x2 -> x0, local copies, waits for them, and re-layouts: 5.36 us -> none  [the longest x1 2.68 us: per_device(): lax.all_gather(local_k, 'blk', axis=0, tiled=True)]
    dot_general x2 -> x0, matrix products: 4.81 us -> none  [the longest x1 3.8 us: fold_step(): jnp.einsum('qhk,khd->qhd', weights, value_heads, preferred_element_type=j...]
    all_to_all x4 -> x0, local copies, waits for them, and re-layouts: 3.62 us -> none  [the longest x1 0.97 us: per_device(): lax.all_to_all(values, 'uly', split_axis=1, concat_axis=0, tiled=True)]
    unnamed x2 -> x7, local copies, waits for them, and re-layouts: 2.5 us -> 3.53 us
  transfers between devices with their start and end apart: 2 -> 0, of which waited for: 2 -> 0; matrix products, arithmetic and copies ran while one was open for 5% -> 0% of each run, Pallas kernels for 0% -> 0%
where the time goes in v1:
time: 53.3 us; the launch traced here: 53.1 us
  Pallas kernels  49.5 us (93%)
  local copies, waits for them, and re-layouts  3.53 us (7%)
    pallas_call x1, Pallas kernels, attend(): pl.pallas_call(attend_kernel, out_shape=jax.ShapeDtypeStruct((rows, featu...  49.5 us
    unnamed x7, local copies, waits for them, and re-layouts  3.53 us

profile of v1, /device:TPU:0, one launch (start us, length us, event | category | flops | bytes accessed | tf_op | source)
XLA Modules:
  0.0 53.1 jit_solution(17902171589898071826)
XLA Ops:
  0.0 0.0 copy-start
  0.0 0.9 %copy-done = bf16[48,2560]{1,0:T(8,128)(2,1)S(1)} copy-done((bf16[48,2560]{1,0:T(8,128)(2,1)S(1)}, bf16[48,2560]{1,0:T(8,128)(2,1)}, u32[]{:S(2)}) %copy-start) | copy-done | bytes 245784
  0.9 0.0 copy-start.1
  0.9 0.9 %copy-done.1 = bf16[48,2560]{1,0:T(8,128)(2,1)S(1)} copy-done((bf16[48,2560]{1,0:T(8,128)(2,1)S(1)}, bf16[48,2560]{1,0:T(8,128)(2,1)}, u32[]{:S(2)}) %copy-start.1) | copy-done | bytes 245784
  1.9 0.0 copy-start.2
  1.9 0.9 %copy-done.2 = bf16[48,2560]{1,0:T(8,128)(2,1)S(1)} copy-done((bf16[48,2560]{1,0:T(8,128)(2,1)S(1)}, bf16[48,2560]{1,0:T(8,128)(2,1)}, u32[]{:S(2)}) %copy-start.2) | copy-done | bytes 245784
  2.8 49.5 %shard_map.37 = bf16[48,2560]{1,0:T(8,128)(2,1)S(1)} custom-call(bf16[48,2560]{1,0:T(8,128)(2,1)S(1)} %copy-done, bf16[48,2560]{1,0:T(8,128)(2,1)S(1)} %copy-done.1, bf16[48,2560]{1,0:T(8,128)(2,1)S(1)} %copy-done.2), custom_call_target="tpu_custom_call" | custom-call | flops 754974720 | bytes 983040 | tf_op jit(solution)/shard_map/pallas_call | solution.py:162
  52.4 0.7 %copy.5 = bf16[48,2560]{1,0:T(8,128)(2,1)} copy(bf16[48,2560]{1,0:T(8,128)(2,1)S(1)} %shard_map.37) | data formatting | bytes 491520
Async XLA Ops:
  0.0 0.9 %copy-start = (bf16[48,2560]{1,0:T(8,128)(2,1)S(1)}, bf16[48,2560]{1,0:T(8,128)(2,1)}, u32[]{:S(2)}) copy-start(bf16[48,2560]{1,0:T(8,128)(2,1)} %q_in.1) | copy-start | bytes 737284
  0.9 0.9 %copy-start.1 = (bf16[48,2560]{1,0:T(8,128)(2,1)S(1)}, bf16[48,2560]{1,0:T(8,128)(2,1)}, u32[]{:S(2)}) copy-start(bf16[48,2560]{1,0:T(8,128)(2,1)} %k_in.1) | copy-start | bytes 737284
  1.9 0.9 %copy-start.2 = (bf16[48,2560]{1,0:T(8,128)(2,1)S(1)}, bf16[48,2560]{1,0:T(8,128)(2,1)}, u32[]{:S(2)}) copy-start(bf16[48,2560]{1,0:T(8,128)(2,1)} %v_in.1) | copy-start | bytes 737284

commit v2 on v1

v2 whole, which is shorter than its diff:
```python
import functools

import jax
import jax.numpy as jnp
from jax import lax
from jax.experimental import pallas as pl
from jax.experimental.pallas import tpu as pltpu
from jax.sharding import PartitionSpec as P

HEAD_DIM = 128
GROUPS = 4
MESH = pl.DeviceIdType.MESH
LOG2E = 1.4426950408889634


def attend_kernel(q_in, k_in, v_in, out, q_buf, kv, o_buf, own_sem, z_send, z_recv, q_recv,
                  x_send, x_recv, y_send, y_recv, s_send, s_recv, d_send, dk_recv, dv_recv,
                  o_send, o_recv):
    rows, features = q_in.shape
    cols = features // GROUPS
    heads = cols // HEAD_DIM
    part = GROUPS * rows
    b, u = lax.axis_index("blk"), lax.axis_index("uly")
    z, y = b // 2, b % 2
    x, c = u // 2, u % 2

    def plane(j):
        return lax.rem(z + j + GROUPS, GROUPS)

    def lanes(h):
        return pl.ds(h * HEAD_DIM, HEAD_DIM)

    def column(index, h):
        return pl.ds(pl.multiple_of(index * cols + h * HEAD_DIM, HEAD_DIM), HEAD_DIM)

    def piece(j):
        return pl.ds(j * rows, rows)

    def slot(s):
        return pl.ds(s * part, part)

    x_peer = (b, 2 * (1 - x) + c)
    y_peer = (2 * z + 1 - y, u)
    sibling = (b, 2 * x + 1 - c)

    def z_peer(j):
        return (2 * plane(j) + y, u)

    sends = []

    def send(src, dst, send_sem, recv_sem, peer):
        copy = pltpu.make_async_remote_copy(
            src_ref=src, dst_ref=dst, send_sem=send_sem, recv_sem=recv_sem,
            device_id=peer, device_id_type=MESH)
        copy.start()
        sends.append(copy)

    def landed(ref, sem):
        pltpu.make_async_copy(ref, ref, sem).wait()

    own = []
    for h in range(heads):
        own.append([
            pltpu.make_async_copy(k_in.at[:, column(z, h)], kv.at[0, piece(0), lanes(h)], own_sem.at[3 * h]),
            pltpu.make_async_copy(v_in.at[:, column(z, h)], kv.at[1, piece(0), lanes(h)], own_sem.at[3 * h + 1]),
            pltpu.make_async_copy(q_in.at[:, column(z, h)], q_buf.at[piece(0), lanes(h)], own_sem.at[3 * h + 2]),
        ])
        for copy in own[h]:
            copy.start()

    barrier = pltpu.get_barrier_semaphore()
    peers = [z_peer(1), z_peer(2), z_peer(3), x_peer, y_peer, sibling]
    for peer in peers:
        pl.semaphore_signal(barrier, inc=1, device_id=peer, device_id_type=MESH)
    pl.semaphore_wait(barrier, len(peers))

    for h in range(heads):
        for j in range(1, GROUPS):
            away, base = column(plane(j), h), 9 * h + 3 * (j - 1)
            send(k_in.at[:, away], kv.at[0, piece(j), lanes(h)], z_send.at[base], z_recv.at[h], z_peer(j))
            send(v_in.at[:, away], kv.at[1, piece(j), lanes(h)], z_send.at[base + 1], z_recv.at[h], z_peer(j))
            send(q_in.at[:, away], q_buf.at[piece(j), lanes(h)], z_send.at[base + 2], q_recv.at[h], z_peer(j))

    def stage1(h):
        for copy in own[h]:
            copy.wait()
        landed(kv.at[:, pl.ds(rows, part - rows), lanes(h)], z_recv.at[h])
        block = kv.at[:, slot(0), lanes(h)]
        send(block, kv.at[:, slot(1), lanes(h)], x_send.at[h], x_recv.at[h], x_peer)
        send(block, kv.at[:, slot(2), lanes(h)], y_send.at[h], y_recv.at[h], y_peer)
        send(block, kv.at[:, slot(4), lanes(h)], s_send.at[4 * h], s_recv.at[h], sibling)

    def stage2(h):
        landed(kv.at[:, slot(1), lanes(h)], x_recv.at[h])
        send(kv.at[0, slot(1), lanes(h)], kv.at[0, slot(3), lanes(h)], d_send.at[2 * h], dk_recv.at[h], y_peer)
        send(kv.at[:, slot(1), lanes(h)], kv.at[:, slot(5), lanes(h)], s_send.at[4 * h + 1], s_recv.at[h], sibling)
        landed(kv.at[:, slot(2), lanes(h)], y_recv.at[h])
        send(kv.at[1, slot(2), lanes(h)], kv.at[1, slot(3), lanes(h)], d_send.at[2 * h + 1], dv_recv.at[h], x_peer)
        send(kv.at[:, slot(2), lanes(h)], kv.at[:, slot(6), lanes(h)], s_send.at[4 * h + 2], s_recv.at[h], sibling)

    def stage3(h):
        landed(kv.at[0, slot(3), lanes(h)], dk_recv.at[h])
        landed(kv.at[1, slot(3), lanes(h)], dv_recv.at[h])
        send(kv.at[:, slot(3), lanes(h)], kv.at[:, slot(7), lanes(h)], s_send.at[4 * h + 3], s_recv.at[h], sibling)

    def fold(h):
        landed(q_buf.at[pl.ds(rows, part - rows), lanes(h)], q_recv.at[h])
        landed(kv.at[:, pl.ds(4 * part, 4 * part), lanes(h)], s_recv.at[h])
        scores = lax.dot_general(
            q_buf[:, lanes(h)], kv[0, :, lanes(h)], (((1,), (1,)), ((), ())),
            preferred_element_type=jnp.float32)
        peak = jnp.max(scores, axis=1, keepdims=True)
        probs = jnp.exp2((scores - peak) * (LOG2E * HEAD_DIM ** -0.5))
        total = jnp.sum(probs, axis=1, keepdims=True)
        summed = jnp.dot(probs.astype(jnp.bfloat16), kv[1, :, lanes(h)],
                         preferred_element_type=jnp.float32)
        o_buf[:, lanes(h)] = (summed / total).astype(jnp.bfloat16)
        for j in range(1, GROUPS):
            send(o_buf.at[piece(j), lanes(h)], out.at[:, column(z, h)],
                 o_send.at[3 * h + j - 1], o_recv.at[j - 1], z_peer(-j))
        keep = pltpu.make_async_copy(o_buf.at[piece(0), lanes(h)], out.at[:, column(z, h)], own_sem.at[3 * h])
        keep.start()
        own[h] = [keep]

    for step in range(heads + 3):
        if step < heads:
            stage1(step)
        if 0 <= step - 1 < heads:
            stage2(step - 1)
        if 0 <= step - 2 < heads:
            stage3(step - 2)
        if 0 <= step - 3 < heads:
            fold(step - 3)

    for h in range(heads):
        for copy in own[h]:
            copy.wait()
    for j in range(1, GROUPS):
        block = pl.ds(pl.multiple_of(plane(j) * cols, HEAD_DIM), cols)
        landed(out.at[:, block], o_recv.at[j - 1])
    for copy in sends:
        copy.wait_send()


def attend(queries, keys, values):
    rows, features = queries.shape
    cols = features // GROUPS
    heads = cols // HEAD_DIM
    part = GROUPS * rows
    dma = pltpu.SemaphoreType.DMA
    flops = 4 * part * cols * 8 * part
    return pl.pallas_call(
        attend_kernel,
        out_shape=jax.ShapeDtypeStruct((rows, features), jnp.bfloat16),
        in_specs=[pl.BlockSpec(memory_space=pl.ANY)] * 3,
        out_specs=pl.BlockSpec(memory_space=pl.ANY),
        scratch_shapes=[
            pltpu.VMEM((part, cols), jnp.bfloat16),
            pltpu.VMEM((2, 8 * part, cols), jnp.bfloat16),
            pltpu.VMEM((part, cols), jnp.bfloat16),
            dma((3 * heads,)), dma((9 * heads,)), dma((heads,)), dma((heads,)),
            dma((heads,)), dma((heads,)), dma((heads,)), dma((heads,)),
            dma((4 * heads,)), dma((heads,)), dma((2 * heads,)), dma((heads,)), dma((heads,)),
            dma((3 * heads,)), dma((3,)),
        ],
        compiler_params=pltpu.CompilerParams(
            collective_id=0, has_side_effects=True, vmem_limit_bytes=60 * 2**20),
        cost_estimate=pl.CostEstimate(flops=flops, bytes_accessed=8 * rows * features, transcendentals=0),
    )(queries, keys, values)


def attend_any(queries, keys, values):
    def to_heads(array):
        return lax.all_to_all(array, "uly", split_axis=1, concat_axis=0, tiled=True)

    heads_q, heads_k, heads_v = to_heads(queries), to_heads(keys), to_heads(values)
    all_k = lax.all_gather(heads_k, "blk", axis=0, tiled=True)
    all_v = lax.all_gather(heads_v, "blk", axis=0, tiled=True)

    def split(array):
        return array.reshape(array.shape[0], -1, HEAD_DIM)

    scores = jnp.einsum("qhd,khd->qhk", split(heads_q), split(all_k),
                        preferred_element_type=jnp.float32) * HEAD_DIM ** (-0.5)
    probs = jnp.exp(scores - jnp.max(scores, axis=2, keepdims=True))
    total = jnp.sum(probs, axis=2)
    summed = jnp.einsum("qhk,khd->qhd", probs.astype(jnp.bfloat16), split(all_v),
                        preferred_element_type=jnp.float32)
    result = (summed / total[:, :, None]).reshape(heads_q.shape).astype(jnp.bfloat16)
    return lax.all_to_all(result, "uly", split_axis=0, concat_axis=1, tiled=True)


def solution(mesh):
    spec = P(("blk", "uly"), None)
    small = mesh.shape["blk"] == 2 * GROUPS and mesh.shape["uly"] == 4
    return jax.shard_map(
        attend if small else attend_any,
        mesh=mesh,
        in_specs=(spec, spec, spec),
        out_specs=spec,
        check_vma=False,
    )
```

time: 53.3 us -> 42.2 us (0.79)
  Pallas kernels: 49.5 us -> 40.3 us
  local copies, waits for them, and re-layouts: 3.53 us -> 1.65 us
    pallas_call x1, Pallas kernels: 49.5 us -> 40.3 us  [attend(): pl.pallas_call(attend_kernel, out_shape=jax.ShapeDtypeStruct((rows, featu...]
    unnamed x7 -> x1, local copies, waits for them, and re-layouts: 3.53 us -> 1.65 us
where the time goes in v2:
time: 42.2 us; the launch traced here: 42 us
  Pallas kernels  40.3 us (95%)
  local copies, waits for them, and re-layouts  1.65 us (4%)
    pallas_call x1, Pallas kernels, attend(): pl.pallas_call(attend_kernel, out_shape=jax.ShapeDtypeStruct((rows, featu...  40.3 us
    unnamed x1, local copies, waits for them, and re-layouts  1.65 us

profile of v2, /device:TPU:0, one launch (start us, length us, event | category | flops | bytes accessed | tf_op | source)
XLA Modules:
  0.0 42.0 jit_solution(3489101082210722360)
XLA Ops:
  0.0 40.3 %shard_map.37 = bf16[48,2560]{1,0:T(8,128)(2,1)} custom-call(bf16[48,2560]{1,0:T(8,128)(2,1)} %q_in.1, bf16[48,2560]{1,0:T(8,128)(2,1)} %k_in.1, bf16[48,2560]{1,0:T(8,128)(2,1)} %v_in.1), custom_call_target="tpu_custom_call" | custom-call | flops 754974720 | bytes 983040 | tf_op jit(solution)/shard_map/pallas_call | solution.py:152
  40.4 1.7 %copy.5 = bf16[48,2560]{1,0:T(8,128)(2,1)} copy(bf16[48,2560]{1,0:T(8,128)(2,1)} %shard_map.37) | data formatting | bytes 491520

commit v3 on v2

v3 whole, which is shorter than its diff:
```python
import functools

import jax
import jax.numpy as jnp
from jax import lax
from jax.experimental import pallas as pl
from jax.experimental.pallas import tpu as pltpu
from jax.sharding import PartitionSpec as P

HEAD_DIM = 128
GROUPS = 4
MESH = pl.DeviceIdType.MESH
LOG2E = 1.4426950408889634


def attend_kernel(q_in, k_in, v_in, out, q_buf, kv, o_buf, own_sem, keep_sem, z_send, z_recv, q_recv,
                  p_send, p_recv, f_send, f_recv, o_send, o_recv):
    rows, features = q_in.shape
    cols = features // GROUPS
    heads = cols // HEAD_DIM
    part = GROUPS * rows
    batches = head_batches(heads)
    b, u = lax.axis_index("blk"), lax.axis_index("uly")
    z, y = b // 2, b % 2
    x, c = u // 2, u % 2

    def plane(j):
        return lax.rem(z + j + GROUPS, GROUPS)

    def lanes(span):
        return pl.ds(span[0] * HEAD_DIM, (span[1] - span[0]) * HEAD_DIM)

    def column(index, span):
        start = pl.multiple_of(index * cols + span[0] * HEAD_DIM, HEAD_DIM)
        return pl.ds(start, (span[1] - span[0]) * HEAD_DIM)

    def piece(j):
        return pl.ds(j * rows, rows)

    others = pl.ds(rows, part - rows)
    x_peer = (b, 2 * (1 - x) + c)
    y_peer = (2 * z + 1 - y, u)
    sibling = (b, 2 * x + 1 - c)

    def z_peer(j):
        return (2 * plane(j) + y, u)

    sends = []

    def send(src, dst, send_sem, recv_sem, peer):
        copy = pltpu.make_async_remote_copy(
            src_ref=src, dst_ref=dst, send_sem=send_sem, recv_sem=recv_sem,
            device_id=peer, device_id_type=MESH)
        copy.start()
        sends.append(copy)

    def landed(ref, sem):
        pltpu.make_async_copy(ref, ref, sem).wait()

    every = (0, heads)
    own = [
        pltpu.make_async_copy(k_in.at[:, column(z, every)], kv.at[0, 0, piece(0)], own_sem.at[0]),
        pltpu.make_async_copy(v_in.at[:, column(z, every)], kv.at[1, 0, piece(0)], own_sem.at[1]),
        pltpu.make_async_copy(q_in.at[:, column(z, every)], q_buf.at[piece(0)], own_sem.at[2]),
    ]
    for copy in own:
        copy.start()

    barrier = pltpu.get_barrier_semaphore()
    peers = [z_peer(1), z_peer(2), z_peer(3), x_peer, y_peer, sibling]
    for peer in peers:
        pl.semaphore_signal(barrier, inc=1, device_id=peer, device_id_type=MESH)
    pl.semaphore_wait(barrier, len(peers))

    def send_keys(h):
        span = (h, h + 1)
        for j in range(1, GROUPS):
            away, base = column(plane(j), span), 9 * h + 3 * (j - 1)
            send(k_in.at[:, away], kv.at[0, 0, piece(j), lanes(span)], z_send.at[base], z_recv.at[h], z_peer(j))
            send(v_in.at[:, away], kv.at[1, 0, piece(j), lanes(span)], z_send.at[base + 1], z_recv.at[h], z_peer(j))

    def send_queries(h):
        span = (h, h + 1)
        for j in range(1, GROUPS):
            away, base = column(plane(j), span), 9 * h + 3 * (j - 1)
            send(q_in.at[:, away], q_buf.at[piece(j), lanes(span)], z_send.at[base + 2], q_recv.at[h], z_peer(j))

    def where(t):
        return (piece(0), lanes(every)) if t == 0 else (others, lanes(batches[t - 1]))

    def spread(t):
        at = where(t)
        if t == 0:
            own[0].wait()
            own[1].wait()
        else:
            landed(kv.at[:, 0, *at], z_recv.at[t - 1])
        for i, peer in ((0, x_peer), (1, y_peer)):
            send(kv.at[:, 0, *at], kv.at[:, i + 1, *at], p_send.at[4 * t + i], p_recv.at[4 * t + i], peer)
        send(kv.at[:, 0, *at], kv.at[:, 4, *at], f_send.at[4 * t], f_recv.at[t], sibling)

    def forward(t):
        at = where(t)
        for i, peer in ((0, y_peer), (1, x_peer)):
            landed(kv.at[:, i + 1, *at], p_recv.at[4 * t + i])
            send(kv.at[i, i + 1, *at], kv.at[i, 3, *at], p_send.at[4 * t + 2 + i], p_recv.at[4 * t + 2 + i], peer)
            send(kv.at[:, i + 1, *at], kv.at[:, i + 5, *at], f_send.at[4 * t + i + 1], f_recv.at[t], sibling)

    def finish(t):
        at = where(t)
        for i in range(2):
            landed(kv.at[i, 3, *at], p_recv.at[4 * t + 2 + i])
        send(kv.at[:, 3, *at], kv.at[:, 7, *at], f_send.at[4 * t + 3], f_recv.at[t], sibling)

    def gathered(t):
        landed(kv.at[:, pl.ds(4, 4), *where(t)], f_recv.at[t])

    keeps = []

    def fold(t):
        span = batches[t]
        if t == 0:
            own[2].wait()
            gathered(0)
        landed(q_buf.at[others, lanes(span)], q_recv.at[t])
        gathered(t + 1)
        for h in range(*span):
            one = lanes((h, h + 1))
            scores = lax.dot_general(
                q_buf[:, one], kv[0, :, :, one].reshape(8 * part, HEAD_DIM), (((1,), (1,)), ((), ())),
                preferred_element_type=jnp.float32)
            peak = jnp.max(scores, axis=1, keepdims=True)
            probs = jnp.exp2((scores - peak) * (LOG2E * HEAD_DIM ** -0.5))
            total = jnp.sum(probs, axis=1, keepdims=True)
            summed = jnp.dot(probs.astype(jnp.bfloat16), kv[1, :, :, one].reshape(8 * part, HEAD_DIM),
                             preferred_element_type=jnp.float32)
            o_buf[:, one] = (summed / total).astype(jnp.bfloat16)
        for j in range(1, GROUPS):
            send(o_buf.at[piece(j), lanes(span)], out.at[:, column(z, span)],
                 o_send.at[3 * t + j - 1], o_recv.at[j - 1], z_peer(-j))
        keep = pltpu.make_async_copy(o_buf.at[piece(0), lanes(span)], out.at[:, column(z, span)], keep_sem.at[t])
        keep.start()
        keeps.append(keep)

    last = heads
    steps = {"k": send_keys, "q": send_queries, "s": spread, "f": forward, "d": finish, "F": fold}
    for step in "k0 s0 k1 k2 k3 k4 q0 q1 q2 q3 q4 s1 s2 f0 s3 f1 s4 f2 d0 s5 f3 d1 f4 d2 F0 f5 d3 F1 d4 F2 d5 F3 F4".split():
        steps[step[0]](int(step[1:]))

    for keep in keeps:
        keep.wait()
    for j in range(1, GROUPS):
        landed(out.at[:, column(plane(j), every)], o_recv.at[j - 1])
    for copy in sends:
        copy.wait_send()


def head_batches(heads):
    return [(h, h + 1) for h in range(heads)]


def attend(queries, keys, values):
    rows, features = queries.shape
    cols = features // GROUPS
    heads = cols // HEAD_DIM
    part = GROUPS * rows
    count = len(head_batches(heads))
    dma = pltpu.SemaphoreType.DMA
    flops = 4 * part * cols * 8 * part
    return pl.pallas_call(
        attend_kernel,
        out_shape=jax.ShapeDtypeStruct((rows, features), jnp.bfloat16),
        in_specs=[pl.BlockSpec(memory_space=pl.ANY)] * 3,
        out_specs=pl.BlockSpec(memory_space=pl.ANY),
        scratch_shapes=[
            pltpu.VMEM((part, cols), jnp.bfloat16),
            pltpu.VMEM((2, 8, part, cols), jnp.bfloat16),
            pltpu.VMEM((part, cols), jnp.bfloat16),
            dma((3,)), dma((count,)), dma((9 * count,)), dma((count,)), dma((count,)),
            dma((4 * count + 4,)), dma((4 * count + 4,)), dma((4 * count + 4,)), dma((count + 1,)),
            dma((3 * count,)), dma((3,)),
        ],
        compiler_params=pltpu.CompilerParams(
            collective_id=0, has_side_effects=True, vmem_limit_bytes=60 * 2**20),
        cost_estimate=pl.CostEstimate(flops=flops, bytes_accessed=8 * rows * features, transcendentals=0),
    )(queries, keys, values)


def attend_any(queries, keys, values):
    def to_heads(array):
        return lax.all_to_all(array, "uly", split_axis=1, concat_axis=0, tiled=True)

    heads_q, heads_k, heads_v = to_heads(queries), to_heads(keys), to_heads(values)
    all_k = lax.all_gather(heads_k, "blk", axis=0, tiled=True)
    all_v = lax.all_gather(heads_v, "blk", axis=0, tiled=True)

    def split(array):
        return array.reshape(array.shape[0], -1, HEAD_DIM)

    scores = jnp.einsum("qhd,khd->qhk", split(heads_q), split(all_k),
                        preferred_element_type=jnp.float32) * HEAD_DIM ** (-0.5)
    probs = jnp.exp(scores - jnp.max(scores, axis=2, keepdims=True))
    total = jnp.sum(probs, axis=2)
    summed = jnp.einsum("qhk,khd->qhd", probs.astype(jnp.bfloat16), split(all_v),
                        preferred_element_type=jnp.float32)
    result = (summed / total[:, :, None]).reshape(heads_q.shape).astype(jnp.bfloat16)
    return lax.all_to_all(result, "uly", split_axis=0, concat_axis=1, tiled=True)


def solution(mesh):
    spec = P(("blk", "uly"), None)
    small = mesh.shape["blk"] == 2 * GROUPS and mesh.shape["uly"] == 4
    return jax.shard_map(
        attend if small else attend_any,
        mesh=mesh,
        in_specs=(spec, spec, spec),
        out_specs=spec,
        check_vma=False,
    )
```

time: 42.2 us -> 37.4 us (0.89)
  Pallas kernels: 40.3 us -> 35.6 us
    pallas_call x1, Pallas kernels: 40.3 us -> 35.6 us  [attend(): pl.pallas_call(attend_kernel, out_shape=jax.ShapeDtypeStruct((rows, featu...]
where the time goes in v3:
time: 37.4 us; the launch traced here: 37.3 us
  Pallas kernels  35.6 us (95%)
  local copies, waits for them, and re-layouts  1.65 us (4%)
    pallas_call x1, Pallas kernels, attend(): pl.pallas_call(attend_kernel, out_shape=jax.ShapeDtypeStruct((rows, featu...  35.6 us
    unnamed x1, local copies, waits for them, and re-layouts  1.65 us

profile of v3, /device:TPU:0, one launch (start us, length us, event | category | flops | bytes accessed | tf_op | source)
XLA Modules:
  0.0 37.3 jit_solution(206653216959598185)
XLA Ops:
  0.0 35.6 %shard_map.37 = bf16[48,2560]{1,0:T(8,128)(2,1)} custom-call(bf16[48,2560]{1,0:T(8,128)(2,1)} %q_in.1, bf16[48,2560]{1,0:T(8,128)(2,1)} %k_in.1, bf16[48,2560]{1,0:T(8,128)(2,1)} %v_in.1), custom_call_target="tpu_custom_call" | custom-call | flops 754974720 | bytes 983040 | tf_op jit(solution)/shard_map/pallas_call | solution.py:170
  35.6 1.7 %copy.5 = bf16[48,2560]{1,0:T(8,128)(2,1)} copy(bf16[48,2560]{1,0:T(8,128)(2,1)} %shard_map.37) | data formatting | bytes 491520

commit v4 on v3

--- a/solution.py
+++ b/solution.py
@@ -40,6 +40,7 @@
     others = pl.ds(rows, part - rows)
     x_peer = (b, 2 * (1 - x) + c)
     y_peer = (2 * z + 1 - y, u)
+    d_peer = (2 * z + 1 - y, 2 * (1 - x) + c)
     sibling = (b, 2 * x + 1 - c)
 
     def z_peer(j):
@@ -67,7 +68,7 @@
         copy.start()
 
     barrier = pltpu.get_barrier_semaphore()
-    peers = [z_peer(1), z_peer(2), z_peer(3), x_peer, y_peer, sibling]
+    peers = [z_peer(1), z_peer(2), z_peer(3), x_peer, y_peer, d_peer, sibling]
     for peer in peers:
         pl.semaphore_signal(barrier, inc=1, device_id=peer, device_id_type=MESH)
     pl.semaphore_wait(barrier, len(peers))
@@ -87,6 +88,9 @@
 
     def where(t):
         return (piece(0), lanes(every)) if t == 0 else (others, lanes(batches[t - 1]))
+
+    def straight(t):
+        return t == heads
 
     def spread(t):
         at = where(t)
@@ -97,18 +101,23 @@
             landed(kv.at[:, 0, *at], z_recv.at[t - 1])
         for i, peer in ((0, x_peer), (1, y_peer)):
             send(kv.at[:, 0, *at], kv.at[:, i + 1, *at], p_send.at[4 * t + i], p_recv.at[4 * t + i], peer)
+        if straight(t):
+            send(kv.at[:, 0, *at], kv.at[:, 3, *at], p_send.at[4 * t + 2], p_recv.at[4 * t + 2], d_peer)
         send(kv.at[:, 0, *at], kv.at[:, 4, *at], f_send.at[4 * t], f_recv.at[t], sibling)
 
     def forward(t):
         at = where(t)
         for i, peer in ((0, y_peer), (1, x_peer)):
             landed(kv.at[:, i + 1, *at], p_recv.at[4 * t + i])
-            send(kv.at[i, i + 1, *at], kv.at[i, 3, *at], p_send.at[4 * t + 2 + i], p_recv.at[4 * t + 2 + i], peer)
+            if not straight(t):
+                send(kv.at[i, i + 1, *at], kv.at[i, 3, *at], p_send.at[4 * t + 2 + i], p_recv.at[4 * t + 2 + i], peer)
             send(kv.at[:, i + 1, *at], kv.at[:, i + 5, *at], f_send.at[4 * t + i + 1], f_recv.at[t], sibling)
 
     def finish(t):
         at = where(t)
-        for i in range(2):
+        if straight(t):
+            landed(kv.at[:, 3, *at], p_recv.at[4 * t + 2])
+        for i in range(0 if straight(t) else 2):
             landed(kv.at[i, 3, *at], p_recv.at[4 * t + 2 + i])
         send(kv.at[:, 3, *at], kv.at[:, 7, *at], f_send.at[4 * t + 3], f_recv.at[t], sibling)
 
@@ -144,7 +153,10 @@
 
     last = heads
     steps = {"k": send_keys, "q": send_queries, "s": spread, "f": forward, "d": finish, "F": fold}
-    for step in "k0 s0 k1 k2 k3 k4 q0 q1 q2 q3 q4 s1 s2 f0 s3 f1 s4 f2 d0 s5 f3 d1 f4 d2 F0 f5 d3 F1 d4 F2 d5 F3 F4".split():
+    order = ("k0", "s0", "k1", "k2", "k3", "k4", "q0", "q1", "q2", "q3", "q4", "s1", "s2",
+             "f0", "s3", "f1", "s4", "f2", "d0", "s5", "f3", "d1", "f4", "d2", "F0", "f5", "d3", "F1",
+             "d4", "d5", "F2", "F3", "F4")
+    for step in order:
         steps[step[0]](int(step[1:]))
 
     for keep in keeps:

time: 37.4 us -> 37 us (0.989)
  Pallas kernels: 35.6 us -> 35.2 us
    pallas_call x1, Pallas kernels: 35.6 us -> 35.2 us  [attend(): pl.pallas_call(attend_kernel, out_shape=jax.ShapeDtypeStruct((rows, featu...]
where the time goes in v4:
time: 37 us; the launch traced here: 36.9 us
  Pallas kernels  35.2 us (95%)
  local copies, waits for them, and re-layouts  1.65 us (4%)
    pallas_call x1, Pallas kernels, attend(): pl.pallas_call(attend_kernel, out_shape=jax.ShapeDtypeStruct((rows, featu...  35.2 us
    unnamed x1, local copies, waits for them, and re-layouts  1.65 us

profile of v4, /device:TPU:0, one launch (start us, length us, event | category | flops | bytes accessed | tf_op | source)
XLA Modules:
  0.0 36.9 jit_solution(11111238063907008064)
XLA Ops:
  0.0 35.2 %shard_map.37 = bf16[48,2560]{1,0:T(8,128)(2,1)} custom-call(bf16[48,2560]{1,0:T(8,128)(2,1)} %q_in.1, bf16[48,2560]{1,0:T(8,128)(2,1)} %k_in.1, bf16[48,2560]{1,0:T(8,128)(2,1)} %v_in.1), custom_call_target="tpu_custom_call" | custom-call | flops 754974720 | bytes 983040 | tf_op jit(solution)/shard_map/pallas_call | solution.py:182
  35.2 1.7 %copy.5 = bf16[48,2560]{1,0:T(8,128)(2,1)} copy(bf16[48,2560]{1,0:T(8,128)(2,1)} %shard_map.37) | data formatting | bytes 491520

commit v5 on v4

--- a/solution.py
+++ b/solution.py
@@ -64,13 +64,12 @@
         pltpu.make_async_copy(v_in.at[:, column(z, every)], kv.at[1, 0, piece(0)], own_sem.at[1]),
         pltpu.make_async_copy(q_in.at[:, column(z, every)], q_buf.at[piece(0)], own_sem.at[2]),
     ]
-    for copy in own:
-        copy.start()
-
     barrier = pltpu.get_barrier_semaphore()
     peers = [z_peer(1), z_peer(2), z_peer(3), x_peer, y_peer, d_peer, sibling]
     for peer in peers:
         pl.semaphore_signal(barrier, inc=1, device_id=peer, device_id_type=MESH)
+    for copy in own:
+        copy.start()
     pl.semaphore_wait(barrier, len(peers))
 
     def send_keys(h):

time: 37 us -> 37 us (level)
  no operation moved by 1% of the time
where the time goes in v5:
time: 37 us; the launch traced here: 36.9 us
  Pallas kernels  35.2 us (95%)
  local copies, waits for them, and re-layouts  1.65 us (4%)
    pallas_call x1, Pallas kernels, attend(): pl.pallas_call(attend_kernel, out_shape=jax.ShapeDtypeStruct((rows, featu...  35.2 us
    unnamed x1, local copies, waits for them, and re-layouts  1.65 us

profile of v5, /device:TPU:0, one launch (start us, length us, event | category | flops | bytes accessed | tf_op | source)
XLA Modules:
  0.0 36.9 jit_solution(15509513079918306065)
XLA Ops:
  0.0 35.2 %shard_map.37 = bf16[48,2560]{1,0:T(8,128)(2,1)} custom-call(bf16[48,2560]{1,0:T(8,128)(2,1)} %q_in.1, bf16[48,2560]{1,0:T(8,128)(2,1)} %k_in.1, bf16[48,2560]{1,0:T(8,128)(2,1)} %v_in.1), custom_call_target="tpu_custom_call" | custom-call | flops 754974720 | bytes 983040 | tf_op jit(solution)/shard_map/pallas_call | solution.py:181
  35.2 1.7 %copy.5 = bf16[48,2560]{1,0:T(8,128)(2,1)} copy(bf16[48,2560]{1,0:T(8,128)(2,1)} %shard_map.37) | data formatting | bytes 491520
